TPU v7x, 32 devices: a whole 2x2x4 slice. The times are simulated.
32 devices in a mesh: section: 8 (over z, y), dp: 4 (over x, core).
Axes of the slice: x: 2, y: 2, z: 4, core: 2. Of those that a mesh axis runs over, the one named last changes fastest.
Arguments:
- w_first: bfloat16 [8, 512, 2048], P('section'), may hold values from -0.25 to 0.25
- w_second_t: bfloat16 [8, 512, 2048], P('section'), may hold values from -0.125 to 0.125
- m_first: float32 [8, 512, 2048], P('section', 'dp'), may hold values from -6 to 6
- v_first: float32 [8, 512, 2048], P('section', 'dp'), may hold values from 10 to 100
- m_second: float32 [8, 512, 2048], P('section', 'dp'), may hold values from -6 to 6
- v_second: float32 [8, 512, 2048], P('section', 'dp'), may hold values from 10 to 100
- lengths: int32 [4, 10], replicated, may hold values from 1 to 256, 1280 in all within a row
- act_arrive: bfloat16 [4, 8, 256, 512], P('dp', 'section'), may hold values from -6 to 6
- cot_arrive: bfloat16 [4, 8, 256, 512], P('dp', 'section'), may hold values from -6 to 6
- embed_next: bfloat16 [4, 2, 256, 512], P('dp'), may hold values from -6 to 6
- loss_cot: bfloat16 [4, 2, 256, 512], P('dp'), may hold values from -6 to 6
- stash: bfloat16 [4, 8, 3, 256, 512], P('dp', 'section'), may hold values from -6 to 6
Outputs:
- act_leave: bfloat16 [4, 8, 3, 256, 512], P('dp', 'section')
- cot_leave: bfloat16 [4, 8, 3, 256, 512], P('dp', 'section')
- step_first: float32 [8, 512, 2048], P('section', 'dp')
- step_second: float32 [8, 512, 2048], P('section', 'dp')
Inputs may be any that keep to these rules, and one draw needn't show every extreme that they name: lengths[g, m] counts the live rows of microbatch m of data group g; each row of lengths sums to 1280 and its largest entry is 256.
All inputs are finite; a program needn't handle non-finite values.
Results may differ from a plain program's by a relative error of at most 0.007.
Values may be sent and summed in bfloat16 or wider, within the bound.
A program may use at most 128 MiB of HBM per device.

v0:
```python
import jax
import jax.numpy as jnp
from jax import lax
from jax.sharding import PartitionSpec as P

TICKS = 3


NORM_EPS = 1e-05
ADAM_EPS = 1e-08
beta_one = 0.9
beta_two = 0.98
correct_one = 1.0 - 0.9**10
correct_two = 1.0 - 0.98**10
gelu_coeff = 0.7978845608
cubic_coeff = 0.044715
residual_alpha = 1500.0**0.25
contract_rows = (((0,), (0,)), ((), ()))
contract_cols = (((1,), (1,)), ((), ()))


def shifted(x, axis, by):
    size = lax.axis_size(axis)
    pairs = [(i, i + by) for i in range(size) if 0 <= i + by < size]
    return lax.ppermute(x, axis, pairs)


def gelu_parts(pre_act):
    inner_arg = gelu_coeff * (pre_act + cubic_coeff * pre_act * pre_act * pre_act)
    tangent = jnp.tanh(inner_arg)
    gelu_value = 0.5 * pre_act * (1.0 + tangent)
    gelu_slope = 0.5 * (1.0 + tangent) + 0.5 * pre_act * (1.0 - tangent * tangent) * gelu_coeff * (
        1.0 + 3.0 * cubic_coeff * pre_act * pre_act
    )
    return (gelu_value, gelu_slope)


def layer_forward(inputs, weight_first, weight_second, residual_scale):
    pre_act = jnp.dot(inputs, weight_first, preferred_element_type=jnp.float32)
    gelu_value, gelu_slope = gelu_parts(pre_act)
    hidden = gelu_value.astype(jnp.bfloat16)
    branch = lax.dot_general(
        hidden, weight_second, contract_cols, preferred_element_type=jnp.float32
    )
    summed = residual_scale * inputs.astype(jnp.float32) + branch
    center = summed - jnp.mean(summed, axis=1, keepdims=True)
    inv_std = lax.rsqrt(jnp.mean(center * center, axis=1, keepdims=True) + NORM_EPS)
    return (gelu_slope, hidden, center * inv_std, inv_std)


def live_mask(inputs, length, first_row):
    return lax.broadcasted_iota(jnp.int32, (inputs.shape[0], 1), 0) + first_row < length


def section_forward(inputs, weight_first, weight_second, length, first_row, residual_scale):
    normed = layer_forward(inputs, weight_first, weight_second, residual_scale)[2]
    return jnp.where(live_mask(inputs, length, first_row), normed, 0.0).astype(jnp.bfloat16)


def section_backward(
    inputs, cotangent, weight_first, weight_second, length, first_row, residual_scale
):
    gelu_slope, hidden, normed, inv_std = layer_forward(
        inputs, weight_first, weight_second, residual_scale
    )
    grad_out = jnp.where(live_mask(inputs, length, first_row), cotangent.astype(jnp.float32), 0.0)
    grad_sum = inv_std * (
        grad_out
        - jnp.mean(grad_out, axis=1, keepdims=True)
        - normed * jnp.mean(grad_out * normed, axis=1, keepdims=True)
    )
    grad_sum_b = grad_sum.astype(jnp.bfloat16)
    grad_hidden = jnp.dot(grad_sum_b, weight_second, preferred_element_type=jnp.float32)
    grad_pre = (grad_hidden * gelu_slope).astype(jnp.bfloat16)
    grad_in = (
        residual_scale * grad_sum
        + lax.dot_general(grad_pre, weight_first, contract_cols, preferred_element_type=jnp.float32)
    ).astype(jnp.bfloat16)
    return (grad_in, grad_pre, grad_sum_b, hidden)


def adam_step(gradient, moment, second):
    moment_new = beta_one * moment + (1.0 - beta_one) * gradient
    second_new = beta_two * second + (1.0 - beta_two) * gradient * gradient
    return moment_new / correct_one / (jnp.sqrt(second_new / correct_two) + ADAM_EPS)


def on_device(
    w_first,
    w_second_t,
    m_first,
    v_first,
    m_second,
    v_second,
    lengths,
    act_arrive,
    cot_arrive,
    embed_next,
    loss_cot,
    stash,
):
    section_id = lax.axis_index("section")
    section_count = lax.axis_size("section")
    group_id = lax.axis_index("dp")
    weight_first = w_first[0]
    weight_second = w_second_t[0]
    group_lengths = lax.dynamic_index_in_dim(lengths, group_id, 0, keepdims=False)
    model_width = weight_first.shape[0]
    hidden_units = weight_first.shape[1]
    inputs = act_arrive[0, 0]
    forward_outs = []
    for tick_index in range(TICKS):
        length = group_lengths[tick_index - section_id + section_count - 1]
        outputs = section_forward(inputs, weight_first, weight_second, length, 0, residual_alpha)
        forward_outs.append(outputs)
        if tick_index + 1 < TICKS:
            passed = shifted(outputs, "section", 1)
            inputs = jnp.where(section_id == 0, embed_next[0, tick_index], passed)
    totals = ()
    cotangent = cot_arrive[0, 0]
    backward_outs = []
    kept_terms = []
    for tick_index in range(TICKS):
        length = group_lengths[tick_index + section_id]
        saved_in = stash[0, 0, tick_index]
        grad_in, tile_grad_pre, tile_grad_sum_b, tile_hidden = section_backward(
            saved_in, cotangent, weight_first, weight_second, length, 0, residual_alpha
        )
        grad_in, totals, stored = (grad_in, totals, (tile_grad_pre, tile_grad_sum_b, tile_hidden))
        backward_outs.append(grad_in)
        kept_terms.append((saved_in, stored))
        if tick_index + 1 < TICKS:
            passed = shifted(grad_in, "section", -1)
            cotangent = jnp.where(section_id == section_count - 1, loss_cot[0, tick_index], passed)
    owned_rows = model_width // lax.axis_size("dp")
    block_first = jnp.zeros((owned_rows * lax.axis_size("dp"), hidden_units), jnp.float32)
    block_second = jnp.zeros((owned_rows * lax.axis_size("dp"), hidden_units), jnp.float32)
    for saved_in, stored in kept_terms:
        grad_pre, grad_sum_b, hidden = stored
        block_first = block_first + lax.dot_general(
            saved_in, grad_pre, contract_rows, preferred_element_type=jnp.float32
        )
        block_second = block_second + lax.dot_general(
            grad_sum_b, hidden, contract_rows, preferred_element_type=jnp.float32
        )
    reduced = lax.psum_scatter(
        jnp.concatenate([block_first, block_second], axis=1).astype(jnp.bfloat16),
        "dp",
        scatter_dimension=0,
        tiled=True,
    ).astype(jnp.float32)
    grad_first = reduced[:, :hidden_units]
    grad_second = reduced[:, hidden_units:]
    step_first = adam_step(grad_first, m_first[0], v_first[0])[None]
    step_second = adam_step(grad_second, m_second[0], v_second[0])[None]
    act_leave = jnp.stack(forward_outs, axis=0)[None, None]
    cot_leave = jnp.stack(backward_outs, axis=0)[None, None]
    return (act_leave, cot_leave, step_first, step_second)


def solution(mesh):
    placed = (
        P("section", None, None),
        P("section", None, None),
        P("section", "dp", None),
        P("section", "dp", None),
        P("section", "dp", None),
        P("section", "dp", None),
        P(),
        P("dp", "section", None, None),
        P("dp", "section", None, None),
        P("dp", None, None, None),
        P("dp", None, None, None),
        P("dp", "section", None, None, None),
    )
    return jax.shard_map(
        on_device,
        mesh=mesh,
        in_specs=placed,
        out_specs=(
            P("dp", "section", None, None, None),
            P("dp", "section", None, None, None),
            P("section", "dp", None),
            P("section", "dp", None),
        ),
        check_vma=False,
    )
```

profile of v0, /device:TPU:0, one launch (start us, length us, event | category | flops | bytes accessed | tf_op | source)
XLA Modules:
  0.0 128.7 jit_solution(15392995297280431553)
XLA Ops:
  7.2 1.5 %fusion.175 = (s32[1,1]{1,0:T(1,128)}, s32[1,1]{1,0:T(1,128)}, s32[1,1]{1,0:T(1,128)}, s32[1,1]{1,0:T(1,128)}, s32[1,1]{1,0:T(1,128)}, /*index=5*/s32[1,1]{1,0:T(1,128)}) fusion(s32[4,10]{1,0:T(4,128)} %param.18, s32[]{:T(128)S(6)} %select_n.78, s32[]{:T(128)S(6)} %select_n.92, s32[]{:T(128)S(6)} %select_n.88, s32[]{:T(128)S(6)} %select_n.83, ...), kind=kLoop, calls=%fused_computation.208 | loop fusion | bytes 76 | tf_op jit(solution)/shard_map/dynamic_slice | solution.py:124
  9.5 2.5 %fusion.59 = f32[256,2048]{1,0:T(8,128)S(1)} fusion(bf16[1,512,2048]{2,1,0:T(8,128)(2,1)} %param.12, bf16[1,1,3,256,512]{4,3,2,1,0:T(8,128)(2,1)} %param.23), kind=kOutput, calls=%fused_computation.74 | convolution fusion | flops 536870912 | bytes 4456448 | tf_op jit(solution)/shard_map/dot_general | solution.py:39
  12.0 1.0 fusion.187
  13.5 2.3 %fusion.1 = bf16[256,2048]{1,0:T(8,128)(2,1)S(1)} fusion(f32[256,2048]{1,0:T(8,128)S(1)} %fusion.59, bf16[1,512,2048]{2,1,0:T(8,128)(2,1)S(1)} %copy-done, f32[256,512]{1,0:T(8,128)S(1)} %get-tuple-element.39, bf16[1,1,256,512]{3,2,1,0:T(8,128)(2,1)S(1)} %copy-done.17, f32[256]{0:T(256)S(1)} %get-tuple-element.40, f32[256]{0:T(256)S(1)} %get-tuple-element.41, ...), kind=kOutput, calls=%fused_computation.16 | convolution fusion | flops 548012032 | bytes 6033664 | tf_op jit(solution)/shard_map/dot_general | solution.py:73
  15.9 0.8 fusion.100
  16.6 1.5 %collective-permute-start.2 = (bf16[256,512]{1,0:T(8,128)(2,1)S(1)}, bf16[256,512]{1,0:T(8,128)(2,1)}, u32[]{:S(2)}, u32[]{:S(2)}) collective-permute-start(bf16[256,512]{1,0:T(8,128)(2,1)S(1)} %fusion.100), channel_id=1, source_target_pairs={{4,0},{8,4},{12,8},{16,12},{20,16},{24,20},{28,24},{5,1},{9,5},{13... | collective-permute-start | bytes 786440 | tf_op jit(solution)/shard_map/ppermute | solution.py:25
  18.1 0.7 fusion.51
  18.9 0.7 fusion.55
  19.6 3.1 %fusion.158 = f32[512,2048]{0,1:T(8,128)} fusion(f32[256,2048]{1,0:T(8,128)S(1)} %fusion.59, f32[256,512]{1,0:T(8,128)S(1)} %get-tuple-element.39, bf16[1,1,256,512]{3,2,1,0:T(8,128)(2,1)S(1)} %copy-done.17, f32[256]{0:T(256)S(1)} %get-tuple-element.40, f32[256]{0:T(256)S(1)} %get-tuple-element.41, f32[256]{0:T(256)S(1)} %add_rsqrt_fusion.2, ...), kind=kOutput, calls=%fused_computation.169 | convolution fusion | flops 542769152 | bytes 7082240 | tf_op jit(solution)/shard_map/dot_general | solution.py:143
  22.7 2.7 %fusion.140 = f32[2048,512]{1,0:T(8,128)} fusion(bf16[256,2048]{1,0:T(8,128)(2,1)S(1)} %fusion.1, bf16[1,1,3,256,512]{4,3,2,1,0:T(8,128)(2,1)S(1)} %copy-done.13), kind=kOutput, calls=%fused_computation.150 | convolution fusion | flops 536870912 | bytes 5505024 | tf_op jit(solution)/shard_map/dot_general | solution.py:140
  26.1 1.0 fusion.185
  27.3 1.0 fusion.186
  29.2 1.3 %fusion.133 = (f32[256]{0:T(256)S(1)}, f32[256]{0:T(256)S(1)}, bf16[256,512]{1,0:T(8,128)(2,1)S(1)}) fusion(pred[256]{0:T(512)(128)(4,1)S(1)} %iota_compare_fusion.1, f32[256]{0:T(256)S(1)} %add_rsqrt_fusion.1, f32[256,512]{1,0:T(8,128)S(1)} %get-tuple-element.37, f32[256]{0:T(256)S(1)} %broadcast_multiply_fusion.5, ...), kind=kLoop, calls=%fused_computation.131 | loop fusion | flops 1048064 | bytes 1315073 | tf_op jit(solution)/shard_map/reduce_sum | solution.py:69
  30.6 3.7 %fusion.2 = bf16[256,2048]{1,0:T(8,128)(2,1)S(1)} fusion(f32[256,2048]{1,0:T(8,128)} %copy-done.6, bf16[1,512,2048]{2,1,0:T(8,128)(2,1)S(1)} %copy-done, bf16[256,512]{1,0:T(8,128)(2,1)S(1)} %get-tuple-element.19, f32[256,512]{1,0:T(8,128)S(1)} %get-tuple-element.37, f32[256]{0:T(256)S(1)} %broadcast_multiply_fusion.3, ...), kind=kOutput, calls=%fused_computation.17 | convolution fusion | flops 548012032 | bytes 6033664 | tf_op jit(solution)/shard_map/dot_general | solution.py:73
  34.2 1.2 fusion.155
  35.8 0.8 fusion.97
  36.6 1.8 %collective-permute-start.3 = (bf16[256,512]{1,0:T(8,128)(2,1)S(1)}, bf16[256,512]{1,0:T(8,128)(2,1)S(1)}, u32[]{:S(2)}, u32[]{:S(2)}) collective-permute-start(bf16[256,512]{1,0:T(8,128)(2,1)S(1)} %fusion.97), channel_id=1, source_target_pairs={{4,0},{8,4},{12,8},{16,12},{20,16},{24,20},{28,24},{5,1},{9,5},{13... | collective-permute-start | bytes 786440 | tf_op jit(solution)/shard_map/ppermute | solution.py:25
  38.4 0.8 fusion.137
  39.2 9.5 %collective-permute-done.3 = bf16[256,512]{1,0:T(8,128)(2,1)S(1)} collective-permute-done((bf16[256,512]{1,0:T(8,128)(2,1)S(1)}, bf16[256,512]{1,0:T(8,128)(2,1)S(1)}, u32[]{:S(2)}, u32[]{:S(2)}) %collective-permute-start.3) | collective-permute-done | bytes 262176 | tf_op jit(solution)/shard_map/ppermute | solution.py:25
  49.1 2.3 %fusion.3 = bf16[256,2048]{1,0:T(8,128)(2,1)S(1)} fusion(f32[256,2048]{1,0:T(8,128)S(1)} %copy-done.9, bf16[1,512,2048]{2,1,0:T(8,128)(2,1)S(1)} %copy-done, bf16[256,512]{1,0:T(8,128)(2,1)S(1)} %get-tuple-element.18, f32[256,512]{1,0:T(8,128)S(1)} %get-tuple-element.35, f32[256]{0:T(256)S(1)} %broadcast_multiply_fusion, ...), kind=kOutput, calls=%fused_computation.18 | convolution fusion | flops 548012032 | bytes 6033664 | tf_op jit(solution)/shard_map/dot_general | solution.py:73
  51.4 1.5 %add_convert_fusion = bf16[512,2048]{0,1:T(8,128)(2,1)S(1)} fusion(f32[512,2048]{0,1:T(8,128)S(1)} %copy-done.5, f32[512,2048]{0,1:T(8,128)S(1)} %fusion.155, f32[256,2048]{1,0:T(8,128)S(1)} %copy-done.9, bf16[256,512]{1,0:T(8,128)(2,1)S(1)} %get-tuple-element.18, f32[256,512]{1,0:T(8,128)S(1)} %get-tuple-element.35, f32[256]{0:T(256)S(1)} %broadcast_multiply_fusion, ...), kind=kOutput, calls=%fused_computation.1 | convolution fusion | flops 545914880 | bytes 13373696 | tf_op jit(solution)/shard_map/dot_general | solution.py:143
  52.9 1.0 copy-done.1
  54.0 0.7 fusion
  54.7 2.2 %pad_maximum_fusion = bf16[512,4096]{0,1:T(8,128)(2,1)} fusion(bf16[512,2048]{0,1:T(8,128)(2,1)S(1)} %add_convert_fusion, bf16[512,2048]{0,1:T(8,128)(2,1)S(1)} %fusion), kind=kLoop, calls=%fused_computation | loop fusion | flops 8388608 | bytes 8388608 | tf_op jit(solution)/shard_map/concatenate | solution.py:147
  57.0 6.4 %copy.37 = bf16[512,4096]{1,0:T(8,128)(2,1)} copy(bf16[512,4096]{0,1:T(8,128)(2,1)} %pad_maximum_fusion) | data formatting | bytes 8388608
  64.3 3.2 %fusion.176 = (f32[256]{0:T(256)S(1)}, f32[256,512]{1,0:T(8,128)S(1)}) fusion(bf16[1,512,2048]{2,1,0:T(8,128)(2,1)S(1)} %copy-done, bf16[1,512,2048]{2,1,0:T(8,128)(2,1)} %param.12, bf16[1,1,256,512]{3,2,1,0:T(8,128)(2,1)S(1)} %copy-done.25), kind=kOutput, calls=%fused_computation.209 | convolution fusion | flops 1078984448 | bytes 4981760 | tf_op jit(solution)/shard_map/dot_general | solution.py:42
  68.0 5.3 %collective-permute-start = (bf16[256,512]{1,0:T(8,128)(2,1)S(1)}, bf16[256,512]{1,0:T(8,128)(2,1)}, u32[]{:S(2)}, u32[]{:S(2)}) collective-permute-start(bf16[256,512]{1,0:T(8,128)(2,1)S(1)} %select_convert_fusion.2), channel_id=1, source_target_pairs={{0,4},{4,8},{8,12},{12,16},{16,20},{20,24},{24,28},{1,5},{5,9},{9,... | collective-permute-start | bytes 786440 | tf_op jit(solution)/shard_map/ppermute | solution.py:25
  73.9 3.3 %collective-permute-done = bf16[256,512]{1,0:T(8,128)(2,1)} collective-permute-done((bf16[256,512]{1,0:T(8,128)(2,1)S(1)}, bf16[256,512]{1,0:T(8,128)(2,1)}, u32[]{:S(2)}, u32[]{:S(2)}) %collective-permute-start) | collective-permute-done | bytes 262176 | tf_op jit(solution)/shard_map/ppermute | solution.py:25
  77.2 1.0 bitcast_select_fusion.3
  78.2 3.9 %fusion.151 = (f32[256]{0:T(256)S(1)}, f32[256,512]{1,0:T(8,128)}) fusion(bf16[256,512]{1,0:T(8,128)(2,1)S(1)} %bitcast_select_fusion.3, bf16[1,512,2048]{2,1,0:T(8,128)(2,1)S(1)} %copy-done, bf16[1,512,2048]{2,1,0:T(8,128)(2,1)} %param.12), kind=kOutput, calls=%fused_computation.162 | convolution fusion | flops 1078984448 | bytes 4981760 | tf_op jit(solution)/shard_map/dot_general | solution.py:42
  82.1 1.2 multiply_reduce_fusion.6
  83.4 2.1 %select_convert_fusion.1 = bf16[256,512]{1,0:T(8,128)(2,1)} fusion(f32[256]{0:T(256)S(1)} %add_rsqrt_fusion.4, f32[256]{0:T(256)S(1)} %broadcast_multiply_fusion.10, pred[256]{0:T(512)(128)(4,1)S(1)} %iota_compare_fusion.4, f32[256,512]{1,0:T(8,128)} %get-tuple-element.31, bf16[256,512]{1,0:T(8,128)(2,1)S(1)} %bitcast_select_fusion.3), kind=kLoop, calls=%fused_computation.137 | loop fusion | flops 917504 | bytes 1050880 | tf_op jit(solution)/shard_map/convert_element_type | solution.py:57
  85.5 4.8 %collective-permute-start.1 = (bf16[256,512]{1,0:T(8,128)(2,1)}, bf16[256,512]{1,0:T(8,128)(2,1)S(1)}, u32[]{:S(2)}, u32[]{:S(2)}) collective-permute-start(bf16[256,512]{1,0:T(8,128)(2,1)} %select_convert_fusion.1), channel_id=1, source_target_pairs={{0,4},{4,8},{8,12},{12,16},{16,20},{20,24},{24,28},{1,5},{5,9},{9,... | collective-permute-start | bytes 786440 | tf_op jit(solution)/shard_map/ppermute | solution.py:25
  91.0 2.5 %copy.31 = f32[1,128,2048]{1,2,0:T(8,128)} copy(f32[1,128,2048]{2,1,0:T(8,128)} %param.17) | data formatting | bytes 2097152 | tf_op args[5]
  93.5 2.6 %copy.30 = f32[1,128,2048]{1,2,0:T(8,128)} copy(f32[1,128,2048]{2,1,0:T(8,128)} %param.16) | data formatting | bytes 2097152 | tf_op args[4]
  96.1 2.6 %copy.29 = f32[1,128,2048]{1,2,0:T(8,128)} copy(f32[1,128,2048]{2,1,0:T(8,128)} %param.15) | data formatting | bytes 2097152 | tf_op args[3]
  98.7 2.5 %copy.25 = f32[1,128,2048]{1,2,0:T(8,128)} copy(f32[1,128,2048]{2,1,0:T(8,128)} %param.14) | data formatting | bytes 2097152 | tf_op args[2]
  101.2 0.9 fusion.196
  102.1 1.0 bitcast_select_fusion.2
  103.1 3.3 %fusion.152 = (f32[256]{0:T(256)S(1)}, f32[256,512]{1,0:T(8,128)S(1)}) fusion(bf16[256,512]{1,0:T(8,128)(2,1)S(1)} %bitcast_select_fusion.2, bf16[1,512,2048]{2,1,0:T(8,128)(2,1)S(1)} %copy-done, bf16[1,512,2048]{2,1,0:T(8,128)(2,1)} %param.12), kind=kOutput, calls=%fused_computation.163 | convolution fusion | flops 1078984448 | bytes 4981760 | tf_op jit(solution)/shard_map/dot_general | solution.py:42
  106.8 2.2 %maximum_bitcast_fusion = bf16[1,1,3,256,512]{4,3,2,1,0:T(8,128)(2,1)} fusion(bf16[1,256,512]{2,1,0:T(8,128)(2,1)S(1)} %fusion.134, bf16[1,256,512]{2,1,0:T(8,128)(2,1)} %bitcast.7, bf16[1,256,512]{2,1,0:T(8,128)(2,1)} %fusion.196), kind=kLoop, calls=%fused_computation.114 | loop fusion | flops 786432 | bytes 1572864 | tf_op jit(solution)/shard_map/broadcast_in_dim | solution.py:156
  109.0 0.8 fusion.103
  110.0 1.0 maximum_bitcast_fusion.1
  111.0 1.6 %copy.38 = bf16[128,4096]{0,1:T(8,128)(2,1)S(1)} copy(bf16[128,4096]{1,0:T(8,128)(2,1)} %reduce-scatter.4.cloned.1.call-done) | data formatting | bytes 2097152
  112.8 1.1 copy-done.10
  114.5 3.5 %fusion.117 = (f32[1,128,2048]{1,2,0:T(8,128)S(1)}, f32[1,128,2048]{1,2,0:T(8,128)}) fusion(f32[1,128,2048]{1,2,0:T(8,128)S(1)} %copy-done.10, f32[128,4096]{0,1:T(8,128)S(1)} %convert_element_type.116, f32[1,128,2048]{1,2,0:T(8,128)S(1)} %copy-done.11, f32[1,128,2048]{1,2,0:T(8,128)S(1)} %copy-done.12, f32[1,128,2048]{1,2,0:T(8,128)} %copy.25), kind=kLoop, calls=%fused_computation.109 | loop fusion | flops 5767168 | bytes 8388608 | tf_op jit(solution)/shard_map/broadcast_in_dim | solution.py:155
  118.0 2.5 %copy.32 = f32[1,128,2048]{2,1,0:T(8,128)} copy(f32[1,128,2048]{1,2,0:T(8,128)} %get-tuple-element.21) | data formatting | bytes 2097152
  120.5 1.3 %copy.33 = f32[1,128,2048]{2,1,0:T(8,128)} copy(f32[1,128,2048]{1,2,0:T(8,128)S(1)} %get-tuple-element.20) | data formatting | bytes 2097152
  (88 shorter events, 7.7 us)
Async XLA Ops:
  7.2 4.8 %copy-start = (bf16[1,512,2048]{2,1,0:T(8,128)(2,1)S(1)}, bf16[1,512,2048]{2,1,0:T(8,128)(2,1)}, u32[]{:S(2)}) copy-start(bf16[1,512,2048]{2,1,0:T(8,128)(2,1)} %param.13) | copy-start | bytes 6291460
  7.2 103.8 %reduce-scatter.4.cloned.1.call-start = ((), (), s32[]{:S(2)}) async-start(), calls=%async_computation.1 | async-start | bytes 5242880
  9.4 2.5 %copy-start.13 = (bf16[1,1,3,256,512]{4,3,2,1,0:T(8,128)(2,1)S(1)}, bf16[1,1,3,256,512]{4,3,2,1,0:T(8,128)(2,1)}, u32[]{:S(2)}) copy-start(bf16[1,1,3,256,512]{4,3,2,1,0:T(8,128)(2,1)} %param.23) | copy-start | bytes 2359300
  11.9 1.3 copy-start.17
  13.5 2.3 %copy-start.2 = (bf16[1,512,2048]{2,1,0:T(8,128)(2,1)S(1)}, bf16[1,512,2048]{2,1,0:T(8,128)(2,1)}, u32[]{:S(2)}) copy-start(bf16[1,512,2048]{2,1,0:T(8,128)(2,1)} %param.12) | copy-start | bytes 6291460
  16.6 2.2 %copy-start.21 = (bf16[256,512]{1,0:T(8,128)(2,1)}, bf16[256,512]{1,0:T(8,128)(2,1)S(1)}, u32[]{:S(2)}) copy-start(bf16[256,512]{1,0:T(8,128)(2,1)S(1)} %fusion.100) | copy-start | bytes 786436
  16.6 12.5 %collective-permute-start.2 = (bf16[256,512]{1,0:T(8,128)(2,1)S(1)}, bf16[256,512]{1,0:T(8,128)(2,1)}, u32[]{:S(2)}, u32[]{:S(2)}) collective-permute-start(bf16[256,512]{1,0:T(8,128)(2,1)S(1)} %fusion.100), channel_id=1, source_target_pairs={{4,0},{8,4},{12,8},{16,12},{20,16},{24,20},{28,24},{5,1},{9,5},{13... | collective-permute-start | bytes 786440 | tf_op jit(solution)/shard_map/ppermute | solution.py:25
  18.9 7.2 %copy-start.8 = (f32[256,2048]{1,0:T(8,128)}, f32[256,2048]{1,0:T(8,128)S(1)}, u32[]{:S(2)}) copy-start(f32[256,2048]{1,0:T(8,128)S(1)} %fusion.51) | copy-start | bytes 6291460
  19.6 7.8 %copy-start.6 = (f32[256,2048]{1,0:T(8,128)}, f32[256,2048]{1,0:T(8,128)S(1)}, u32[]{:S(2)}) copy-start(f32[256,2048]{1,0:T(8,128)S(1)} %fusion.55) | copy-start | bytes 6291460
  30.5 3.7 %copy-start.7 = (f32[256,2048]{1,0:T(8,128)S(1)}, f32[256,2048]{1,0:T(8,128)}, u32[]{:S(2)}) copy-start(f32[256,2048]{1,0:T(8,128)} %copy-done.6) | copy-start | bytes 6291460
  34.2 1.6 %copy-start.3 = (bf16[1,512,2048]{2,1,0:T(8,128)(2,1)S(1)}, bf16[1,512,2048]{2,1,0:T(8,128)(2,1)}, u32[]{:S(2)}) copy-start(bf16[1,512,2048]{2,1,0:T(8,128)(2,1)} %param.12) | copy-start | bytes 6291460
  35.8 2.6 %copy-start.14 = (bf16[1,1,3,256,512]{4,3,2,1,0:T(8,128)(2,1)S(1)}, bf16[1,1,3,256,512]{4,3,2,1,0:T(8,128)(2,1)}, u32[]{:S(2)}) copy-start(bf16[1,1,3,256,512]{4,3,2,1,0:T(8,128)(2,1)} %param.23) | copy-start | bytes 2359300
  36.6 2.6 %copy-start.23 = (bf16[256,512]{1,0:T(8,128)(2,1)}, bf16[256,512]{1,0:T(8,128)(2,1)S(1)}, u32[]{:S(2)}) copy-start(bf16[256,512]{1,0:T(8,128)(2,1)S(1)} %fusion.97) | copy-start | bytes 786436
  36.6 12.1 %copy-start.20 = (bf16[1,2,256,512]{3,2,1,0:T(8,128)(2,1)S(1)}, bf16[1,2,256,512]{3,2,1,0:T(8,128)(2,1)}, u32[]{:S(2)}) copy-start(bf16[1,2,256,512]{3,2,1,0:T(8,128)(2,1)} %param.22) | copy-start | bytes 1572868
  36.6 12.4 %copy-start.9 = (f32[256,2048]{1,0:T(8,128)S(1)}, f32[256,2048]{1,0:T(8,128)}, u32[]{:S(2)}) copy-start(f32[256,2048]{1,0:T(8,128)} %copy-done.8) | copy-start | bytes 6291460
  36.6 12.1 %collective-permute-start.3 = (bf16[256,512]{1,0:T(8,128)(2,1)S(1)}, bf16[256,512]{1,0:T(8,128)(2,1)S(1)}, u32[]{:S(2)}, u32[]{:S(2)}) collective-permute-start(bf16[256,512]{1,0:T(8,128)(2,1)S(1)} %fusion.97), channel_id=1, source_target_pairs={{4,0},{8,4},{12,8},{16,12},{20,16},{24,20},{28,24},{5,1},{9,5},{13... | collective-permute-start | bytes 786440 | tf_op jit(solution)/shard_map/ppermute | solution.py:25
  49.0 2.4 %copy-start.18 = (bf16[256,512]{1,0:T(8,128)(2,1)}, bf16[256,512]{1,0:T(8,128)(2,1)S(1)}, u32[]{:S(2)}) copy-start(bf16[256,512]{1,0:T(8,128)(2,1)S(1)} %get-tuple-element.18) | copy-start | bytes 786436
  49.1 2.3 %copy-start.5 = (f32[512,2048]{0,1:T(8,128)S(1)}, f32[512,2048]{0,1:T(8,128)}, u32[]{:S(2)}) copy-start(f32[512,2048]{0,1:T(8,128)} %fusion.158) | copy-start | bytes 12582916
  51.4 1.5 %copy-start.15 = (bf16[256,2048]{1,0:T(8,128)(2,1)}, bf16[256,2048]{1,0:T(8,128)(2,1)S(1)}, u32[]{:S(2)}) copy-start(bf16[256,2048]{1,0:T(8,128)(2,1)S(1)} %fusion.3) | copy-start | bytes 3145732
  51.4 2.6 %copy-start.1 = (f32[2048,512]{1,0:T(8,128)S(1)}, f32[2048,512]{1,0:T(8,128)}, u32[]{:S(2)}) copy-start(f32[2048,512]{1,0:T(8,128)} %fusion.140) | copy-start | bytes 12582916
  63.4 1.0 copy-start.25
  68.0 9.2 %collective-permute-start = (bf16[256,512]{1,0:T(8,128)(2,1)S(1)}, bf16[256,512]{1,0:T(8,128)(2,1)}, u32[]{:S(2)}, u32[]{:S(2)}) collective-permute-start(bf16[256,512]{1,0:T(8,128)(2,1)S(1)} %select_convert_fusion.2), channel_id=1, source_target_pairs={{0,4},{4,8},{8,12},{12,16},{16,20},{20,24},{24,28},{1,5},{5,9},{9,... | collective-permute-start | bytes 786440 | tf_op jit(solution)/shard_map/ppermute | solution.py:25
  85.5 16.6 %collective-permute-start.1 = (bf16[256,512]{1,0:T(8,128)(2,1)}, bf16[256,512]{1,0:T(8,128)(2,1)S(1)}, u32[]{:S(2)}, u32[]{:S(2)}) collective-permute-start(bf16[256,512]{1,0:T(8,128)(2,1)} %select_convert_fusion.1), channel_id=1, source_target_pairs={{0,4},{4,8},{8,12},{12,16},{16,20},{20,24},{24,28},{1,5},{5,9},{9,... | collective-permute-start | bytes 786440 | tf_op jit(solution)/shard_map/ppermute | solution.py:25
  106.3 2.6 %copy-start.4 = (bf16[1,512,2048]{2,1,0:T(8,128)(2,1)S(1)}, bf16[1,512,2048]{2,1,0:T(8,128)(2,1)}, u32[]{:S(2)}) copy-start(bf16[1,512,2048]{2,1,0:T(8,128)(2,1)} %param.12) | copy-start | bytes 6291460
  106.3 2.6 %copy-start.16 = (bf16[256,2048]{1,0:T(8,128)(2,1)S(1)}, bf16[256,2048]{1,0:T(8,128)(2,1)}, u32[]{:S(2)}) copy-start(bf16[256,2048]{1,0:T(8,128)(2,1)} %copy-done.15) | copy-start | bytes 3145732
  106.3 2.6 %copy-start.19 = (bf16[256,512]{1,0:T(8,128)(2,1)S(1)}, bf16[256,512]{1,0:T(8,128)(2,1)}, u32[]{:S(2)}) copy-start(bf16[256,512]{1,0:T(8,128)(2,1)} %copy-done.18) | copy-start | bytes 786436
  109.0 1.0 copy-start.22
  109.0 1.0 copy-start.24
  112.6 1.2 copy-start.10
  112.6 1.5 %copy-start.11 = (f32[1,128,2048]{1,2,0:T(8,128)S(1)}, f32[1,128,2048]{1,2,0:T(8,128)}, u32[]{:S(2)}) copy-start(f32[1,128,2048]{1,2,0:T(8,128)} %copy.30) | copy-start | bytes 3145732
  112.6 1.8 %copy-start.12 = (f32[1,128,2048]{1,2,0:T(8,128)S(1)}, f32[1,128,2048]{1,2,0:T(8,128)}, u32[]{:S(2)}) copy-start(f32[1,128,2048]{1,2,0:T(8,128)} %copy.29) | copy-start | bytes 3145732
Sparse Core Ops, SparseCore 0:
  63.5 46.1 reduce-scatter.3
where the time goes:
time: 130 us; the launch traced here: 129 us
  matrix products  38 us (29%)
  local copies, waits for them, and re-layouts  27.3 us (21%)
  other arithmetic  22.4 us (17%)
  between operations  14.7 us (11%)
  starting transfers between devices  13.4 us (10%)
  waiting for transfers between devices  12.8 us (10%)
    unnamed x60, local copies, waits for them, and re-layouts  25.8 us
    dot_general x6, matrix products, layer_forward(): lax.dot_general(hidden, weight_second, contract_cols, preferred_element_t...  13.5 us
    ppermute x4, starting transfers between devices, shifted(): return lax.ppermute(x, axis, pairs)  13.3 us
    ppermute x4, waiting for transfers between devices, shifted(): return lax.ppermute(x, axis, pairs)  12.8 us
    dot_general x3, matrix products, section_backward(): jnp.dot(grad_sum_b, weight_second, preferred_element_type=jnp.float32)  8.27 us
    dot_general x3, matrix products, on_device(): lax.dot_general(grad_sum_b, hidden, contract_rows, preferred_element_type...  5.81 us
    dot_general x3, matrix products, on_device(): lax.dot_general(saved_in, grad_pre, contract_rows, preferred_element_type...  4.21 us
    dot_general x3, matrix products, layer_forward(): pre_act = jnp.dot(inputs, weight_first, preferred_element_type=jnp.float32)  3.87 us
  transfers between devices with their start and end apart: 5, of which 2 were waited for; matrix products, arithmetic and copies ran while one was open for 35% of the time, Pallas kernels for 0%

commit v1 on v0

v1 whole, which is shorter than its diff:
```python
import functools

import jax
import jax.numpy as jnp
from jax import lax
from jax.experimental import pallas as pl
from jax.experimental.pallas import tpu as pltpu
from jax.sharding import PartitionSpec as P

NORM_EPS = 1e-05
ADAM_EPS = 1e-08
beta_one = 0.9
beta_two = 0.98
correct_one = 1.0 - 0.9**10
correct_two = 1.0 - 0.98**10
gelu_coeff = 0.7978845608
cubic_coeff = 0.044715
residual_alpha = 1500.0**0.25
NT = (((1,), (1,)), ((), ()))
BF = jnp.bfloat16
F32 = jnp.float32
MESH = pl.DeviceIdType.MESH


def gelu(pre, slope):
    square = pre * pre
    tangent = jnp.tanh(pre * (gelu_coeff + (gelu_coeff * cubic_coeff) * square))
    half = 0.5 * pre
    cdf = 1.0 + tangent
    hidden = (half * cdf).astype(BF)
    if not slope:
        return hidden, None
    bent = gelu_coeff + (3.0 * gelu_coeff * cubic_coeff) * square
    return hidden, 0.5 * cdf + (half * bent) * (1.0 - tangent * tangent)


def dot(a, b):
    return jnp.dot(a, b, preferred_element_type=F32)


def dot_nt(a, b):
    return lax.dot_general(a, b, NT, preferred_element_type=F32)


def kernel(
    sections, groups, ticks, chunk,
    w1_h, w2_h, m1_h, v1_h, m2_h, v2_h, lengths, act_h, cot_h, embed_h, loss_h, stash_h,
    act_o, cot_o, s1_o, s2_o,
    w1, w2, moments, x_in, a_in, c_in, r_x, r_g, act_b, cot_b, g_b, slopes, normed, inv_std,
    f_hid, hid, gp, xt, gt, acc, out_x, in_x, steps,
    w_sem, mom_sem, x_sem, a_sem, c_sem, o_sem, st_sem,
    hop_s, hop_r, rx_s, rx_r, rg_s, rg_r, ex_s, ex_r,
):
    s = lax.axis_index("section")
    me = lax.axis_index("dp")
    chips = groups // 2
    chip, core = me // 2, me % 2
    sibling = me + 1 - 2 * core
    width, units = w1.shape
    cap = x_in.shape[1]
    rows = width // chips
    own = rows // 2
    chunks = units // chunk
    first, last = s == 0, s == sections - 1
    nxt = jnp.minimum(s + 1, sections - 1)
    prv = jnp.maximum(s - 1, 0)
    partners = [lax.rem(chip + p, chips) * 2 + core for p in range(1, chips)]

    barrier = pltpu.get_barrier_semaphore()

    @pl.when(jnp.logical_not(first))
    def _():
        pl.semaphore_signal(barrier, inc=1, device_id={"section": prv}, device_id_type=MESH)

    @pl.when(jnp.logical_not(last))
    def _():
        pl.semaphore_signal(barrier, inc=1, device_id={"section": nxt}, device_id_type=MESH)

    for other in partners + [sibling]:
        pl.semaphore_signal(barrier, inc=1, device_id={"dp": other}, device_id_type=MESH)

    loads_x = [pltpu.make_async_copy(stash_h.at[0, 0, k], x_in.at[k], x_sem.at[k]) for k in range(ticks)]
    load_w1 = pltpu.make_async_copy(w1_h.at[0], w1, w_sem.at[0])
    load_w2 = pltpu.make_async_copy(w2_h.at[0], w2, w_sem.at[1])
    loads_a = [pltpu.make_async_copy(act_h.at[0, 0], a_in.at[0], a_sem.at[0])]
    loads_c = [pltpu.make_async_copy(cot_h.at[0, 0], c_in.at[0], c_sem.at[0])]
    for k in range(1, ticks):
        loads_a.append(pltpu.make_async_copy(embed_h.at[0, k - 1], a_in.at[k], a_sem.at[k]))
        loads_c.append(pltpu.make_async_copy(loss_h.at[0, k - 1], c_in.at[k], c_sem.at[k]))
    loads_m = [
        pltpu.make_async_copy(h.at[0], moments.at[i], mom_sem.at[i])
        for i, h in enumerate((m1_h, v1_h, m2_h, v2_h))
    ]
    loads_x[0].start()
    load_w1.start()
    load_w2.start()
    loads_c[0].start()
    loads_a[0].start()
    for k in range(1, ticks):
        loads_x[k].start()

    @pl.when(first)
    def _():
        for k in range(1, ticks):
            loads_a[k].start()

    @pl.when(last)
    def _():
        for k in range(1, ticks):
            loads_c[k].start()

    for load in loads_m:
        load.start()

    pl.semaphore_wait(
        barrier, chips + jnp.where(first, 0, 1) + jnp.where(last, 0, 1)
    )

    def send_tick(k, src, dst, send, recv):
        return [
            pltpu.make_async_remote_copy(
                src_ref=src, dst_ref=dst.at[k, p], send_sem=send.at[k, p], recv_sem=recv.at[k, p],
                device_id={"dp": other}, device_id_type=MESH,
            )
            for p, other in enumerate(partners)
        ]

    sends_x = [send_tick(k, stash_h.at[0, 0, k], r_x, rx_s, rx_r) for k in range(ticks)]
    sends_g = [send_tick(k, g_b.at[k], r_g, rg_s, rg_r) for k in range(ticks)]
    for copies in sends_x:
        for copy in copies:
            copy.start()

    def hop(src, dst, i, to):
        return pltpu.make_async_remote_copy(
            src_ref=src, dst_ref=dst, send_sem=hop_s.at[i], recv_sem=hop_r.at[i],
            device_id={"section": to}, device_id_type=MESH,
        )

    hops_a = [hop(act_b.at[k], a_in.at[k + 1], k, nxt) for k in range(ticks - 1)]
    hops_c = [hop(cot_b.at[k], c_in.at[k + 1], ticks - 1 + k, prv) for k in range(ticks - 1)]
    outs_a = [pltpu.make_async_copy(act_b.at[k], act_o.at[k], o_sem.at[k]) for k in range(ticks)]
    outs_c = [pltpu.make_async_copy(cot_b.at[k], cot_o.at[k], o_sem.at[ticks + k]) for k in range(ticks)]

    row_ids = lax.broadcasted_iota(jnp.int32, (cap, 1), 0)
    cols = lambda j: pl.ds(pl.multiple_of(j * chunk, chunk), chunk)
    chip_cols = pl.ds(pl.multiple_of(chip * rows, rows), rows)

    def norm(x, branch):
        summed = residual_alpha * x.astype(F32) + branch
        center = summed - jnp.mean(summed, axis=1, keepdims=True)
        inv = lax.rsqrt(jnp.mean(center * center, axis=1, keepdims=True) + NORM_EPS)
        return center * inv, inv

    def forward(k):
        if k == 0:
            loads_a[0].wait()
        else:
            @pl.when(first)
            def _():
                loads_a[k].wait()

            @pl.when(jnp.logical_not(first))
            def _():
                hops_a[k - 1].wait_recv()

        def body(j, _):
            f_hid[:, cols(j)] = gelu(dot(a_in[k], w1[:, cols(j)]), False)[0]
            return 0

        lax.fori_loop(0, chunks, body, 0)
        value = norm(a_in[k], dot_nt(f_hid[...], w2[...]))[0]
        live = row_ids < lengths[me, k - s + sections - 1]
        act_b[k] = jnp.where(live, value, 0.0).astype(BF)
        if k + 1 < ticks:
            @pl.when(jnp.logical_not(last))
            def _():
                hops_a[k].start()
        outs_a[k].start()

    def block(k):
        return pl.ds(k * cap, cap)

    def stage_a(k):
        loads_x[k].wait()
        if k == 0:
            load_w1.wait()

        def body(j, _):
            hidden, slope = gelu(dot(x_in[k], w1[:, cols(j)]), True)
            hid[block(k), cols(j)] = hidden
            slopes[k, :, cols(j)] = slope
            return 0

        lax.fori_loop(0, chunks, body, 0)
        if k == 0:
            load_w2.wait()
        value, inv = norm(x_in[k], dot_nt(hid[block(k), :], w2[...]))
        normed[k] = value
        inv_std[k] = inv
        xt[:, block(k)] = x_in[k, :, chip_cols].T

    def stage_b(k):
        if k == 0:
            loads_c[0].wait()
        else:
            @pl.when(last)
            def _():
                loads_c[k].wait()

            @pl.when(jnp.logical_not(last))
            def _():
                hops_c[k - 1].wait_recv()

        live = row_ids < lengths[me, k + s]
        grad_out = jnp.where(live, c_in[k].astype(F32), 0.0)
        value = normed[k]
        grad_sum = inv_std[k] * (
            grad_out
            - jnp.mean(grad_out, axis=1, keepdims=True)
            - value * jnp.mean(grad_out * value, axis=1, keepdims=True)
        )
        g_b[k] = grad_sum.astype(BF)
        for copy in sends_g[k]:
            copy.start()
        normed[k] = grad_sum

        def body(j, _):
            gp[block(k), cols(j)] = (dot(g_b[k], w2[:, cols(j)]) * slopes[k, :, cols(j)]).astype(BF)
            return 0

        lax.fori_loop(0, chunks, body, 0)
        cot_b[k] = (residual_alpha * normed[k] + dot_nt(gp[block(k), :], w1[...])).astype(BF)
        if k + 1 < ticks:
            @pl.when(jnp.logical_not(first))
            def _():
                hops_c[k].start()
        outs_c[k].start()
        gt[:, block(k)] = g_b[k, :, chip_cols].T

    def stage_r(k):
        for p in range(chips - 1):
            sends_x[k][p].wait_recv()
            sends_g[k][p].wait_recv()
            place = block(ticks + k * (chips - 1) + p)

            def body(j, _):
                hidden, slope = gelu(dot(r_x[k, p], w1[:, cols(j)]), True)
                hid[place, cols(j)] = hidden
                gp[place, cols(j)] = (dot(r_g[k, p], w2[:, cols(j)]) * slope).astype(BF)
                return 0

            lax.fori_loop(0, chunks, body, 0)
            xt[:, place] = r_x[k, p, :, chip_cols].T
            gt[:, place] = r_g[k, p, :, chip_cols].T

    early = (ticks + (ticks - 1) * (chips - 1)) * cap
    terms = ((xt, gp), (gt, hid))

    stage_a(0)
    stage_b(0)
    forward(0)
    for k in range(1, ticks):
        stage_a(k)
    for k in range(1, ticks):
        stage_b(k)
        stage_r(k - 1)
        forward(k)

    for i, (left, right) in enumerate(terms):
        def body(j, _):
            acc[i, :, cols(j)] = dot(left[:, :early], right[:early, cols(j)])
            return 0

        lax.fori_loop(0, chunks, body, 0)

    stage_r(ticks - 1)

    swaps = []
    theirs = pl.ds(pl.multiple_of((1 - core) * own, own), own)
    mine = pl.ds(pl.multiple_of(core * own, own), own)
    for j in range(chunks):
        span = slice(j * chunk, (j + 1) * chunk)
        for i, (left, right) in enumerate(terms):
            if chips > 1:
                acc[i, :, span] += dot(left[:, early:], right[early:, span])
            out_x[j, i] = acc[i, theirs, span].astype(BF)
        swap = pltpu.make_async_remote_copy(
            src_ref=out_x.at[j], dst_ref=in_x.at[j], send_sem=ex_s.at[j], recv_sem=ex_r.at[j],
            device_id={"dp": sibling}, device_id_type=MESH,
        )
        swap.start()
        swaps.append(swap)
    for load in loads_m:
        load.wait()
    stores = []
    for j in range(chunks):
        span = slice(j * chunk, (j + 1) * chunk)
        swaps[j].wait_recv()
        for i, out in enumerate((s1_o, s2_o)):
            grad = acc[i, mine, span] + in_x[j, i].astype(F32)
            moment = beta_one * moments[2 * i, :, span] + (1.0 - beta_one) * grad
            second = beta_two * moments[2 * i + 1, :, span] + (1.0 - beta_two) * grad * grad
            steps[i, :, span] = (moment * (1.0 / correct_one)) / (
                jnp.sqrt(second * (1.0 / correct_two)) + ADAM_EPS
            )
            store = pltpu.make_async_copy(steps.at[i, :, span], out.at[:, span], st_sem.at[j, i])
            store.start()
            stores.append(store)

    for swap in swaps:
        swap.wait_send()
    for copies in sends_x + sends_g:
        for copy in copies:
            copy.wait_send()

    @pl.when(jnp.logical_not(last))
    def _():
        for copy in hops_a:
            copy.wait_send()

    @pl.when(jnp.logical_not(first))
    def _():
        for copy in hops_c:
            copy.wait_send()

    for store in stores + outs_a + outs_c:
        store.wait()


def on_device(*args):
    w_first, lengths, stash = args[0], args[6], args[11]
    sections, groups = lax.axis_size("section"), lax.axis_size("dp")
    ticks, cap, width = stash.shape[2:]
    units = w_first.shape[2]
    chips = groups // 2
    rows, own = width // chips, width // groups
    chunk = 512 if units % 512 == 0 else units
    chunks = units // chunk
    depth = ticks * chips * cap
    dma = pltpu.SemaphoreType.DMA
    vmem = pltpu.VMEM
    remote = (ticks, max(chips - 1, 1))
    anywhere = pl.BlockSpec(memory_space=pl.ANY)
    leave = jax.ShapeDtypeStruct((ticks, cap, width), BF)
    step = jax.ShapeDtypeStruct((own, units), F32)
    act, cot, step_first, step_second = pl.pallas_call(
        functools.partial(kernel, sections, groups, ticks, chunk),
        out_shape=(leave, leave, step, step),
        in_specs=[anywhere] * 6 + [pl.BlockSpec(memory_space=pltpu.SMEM)] + [anywhere] * 5,
        out_specs=(anywhere,) * 4,
        scratch_shapes=[
            vmem((width, units), BF),
            vmem((width, units), BF),
            vmem((4, own, units), F32),
            vmem((ticks, cap, width), BF),
            vmem((ticks, cap, width), BF),
            vmem((ticks, cap, width), BF),
            vmem(remote + (cap, width), BF),
            vmem(remote + (cap, width), BF),
            vmem((ticks, cap, width), BF),
            vmem((ticks, cap, width), BF),
            vmem((ticks, cap, width), BF),
            vmem((ticks, cap, units), F32),
            vmem((ticks, cap, width), F32),
            vmem((ticks, cap, 1), F32),
            vmem((cap, units), BF),
            vmem((depth, units), BF),
            vmem((depth, units), BF),
            vmem((rows, depth), BF),
            vmem((rows, depth), BF),
            vmem((2, rows, units), F32),
            vmem((chunks, 2, own, chunk), BF),
            vmem((chunks, 2, own, chunk), BF),
            vmem((2, own, units), F32),
            dma((2,)),
            dma((4,)),
            dma((ticks,)),
            dma((ticks,)),
            dma((ticks,)),
            dma((2 * ticks,)),
            dma((chunks, 2)),
            dma((2 * ticks,)),
            dma((2 * ticks,)),
            dma(remote),
            dma(remote),
            dma(remote),
            dma(remote),
            dma((chunks,)),
            dma((chunks,)),
        ],
        compiler_params=pltpu.CompilerParams(
            collective_id=0, has_side_effects=True, vmem_limit_bytes=60 * 2**20
        ),
    )(*args)
    return act[None, None], cot[None, None], step_first[None], step_second[None]


def solution(mesh):
    weight, state = P("section", None, None), P("section", "dp", None)
    block, stack = P("dp", "section", None, None), P("dp", "section", None, None, None)
    group = P("dp", None, None, None)
    return jax.shard_map(
        on_device,
        mesh=mesh,
        in_specs=(weight, weight, state, state, state, state, P(), block, block, group, group, stack),
        out_specs=(stack, stack, state, state),
        check_vma=False,
    )
```

time: 130 us -> 59.7 us (0.46)
  Pallas kernels: 0 us -> 52.5 us
  matrix products: 38 us -> 0 us
  other arithmetic: 22.4 us -> 0 us
  local copies, waits for them, and re-layouts: 27.3 us -> 6.25 us
  between operations: 14.7 us -> 0.66 us
  starting transfers between devices: 13.4 us -> 0 us
  waiting for transfers between devices: 12.8 us -> 0 us
    pallas_call x0 -> x1, Pallas kernels: none -> 52.5 us  [on_device(): pl.pallas_call(functools.partial(kernel, sections, groups, ticks, chunk),...]
    dot_general x21 -> x0, matrix products: 38 us -> none  [the longest x6 13.5 us: layer_forward(): lax.dot_general(hidden, weight_second, contract_cols, preferred_element_t...]
    unnamed x60 -> x8, local copies, waits for them, and re-layouts: 25.8 us -> 6.25 us
    ppermute x4 -> x0, starting transfers between devices: 13.3 us -> none  [shifted(): return lax.ppermute(x, axis, pairs)]
    ppermute x4 -> x0, waiting for transfers between devices: 12.8 us -> none  [shifted(): return lax.ppermute(x, axis, pairs)]
    broadcast_in_dim x3 -> x0, other arithmetic: 6.66 us -> none  [the longest x1 3.49 us: on_device(): step_second = adam_step(grad_second, m_second[0], v_second[0])[None]]
    reduce_sum x9 -> x0, other arithmetic: 4.18 us -> none  [the longest x6 2.25 us: layer_forward(): jnp.mean(center * center, axis=1, keepdims=True) + NORM_EPS]
    lt x6 -> x0, other arithmetic: 3.84 us -> none  [live_mask(): lax.broadcasted_iota(jnp.int32, (inputs.shape[0], 1), 0) + first_row]
  transfers between devices with their start and end apart: 5 -> 0, of which waited for: 2 -> 0; matrix products, arithmetic and copies ran while one was open for 35% -> 0% of each run, Pallas kernels for 0% -> 0%
where the time goes in v1:
time: 59.7 us; the launch traced here: 59.4 us
  Pallas kernels  52.5 us (88%)
  local copies, waits for them, and re-layouts  6.25 us (10%)
  between operations  0.66 us (1%)
    pallas_call x1, Pallas kernels, on_device(): pl.pallas_call(functools.partial(kernel, sections, groups, ticks, chunk),...  52.5 us
    unnamed x8, local copies, waits for them, and re-layouts  6.25 us

profile of v1, /device:TPU:0, one launch (start us, length us, event | category | flops | bytes accessed | tf_op | source)
XLA Modules:
  0.0 59.4 jit_solution(1200148591935935764)
XLA Ops:
  0.6 52.5 %shard_map.147 = (bf16[3,256,512]{2,1,0:T(8,128)(2,1)}, bf16[3,256,512]{2,1,0:T(8,128)(2,1)}, f32[128,2048]{1,0:T(8,128)}, f32[128,2048]{1,0:T(8,128)}) custom-call(bf16[1,512,2048]{2,1,0:T(8,128)(2,1)} %w1_h.1, bf16[1,512,2048]{2,1,0:T(8,128)(2,1)} %w2_h.1, f32[1,128,2048]{2,1,0:T(8,128)} %m1_h.1, f32[1,128,2048]{2,1,0:T(8,128)} %v1_h.1, ...), custom_call_target="tpu_custom_call" | custom-call | tf_op jit(solution)/shard_map/pallas_call | solution.py:347
  53.1 0.0 copy-start.1
  53.1 2.2 %copy.20 = bf16[1,1,3,256,512]{4,3,2,1,0:T(8,128)(2,1)} copy(bf16[1,1,3,256,512]{4,3,2,1,0:T(8,128)(2,1)} %bitcast.7) | data formatting | bytes 1572864
  55.3 0.0 copy-start
  55.3 2.2 %copy.21 = bf16[1,1,3,256,512]{4,3,2,1,0:T(8,128)(2,1)} copy(bf16[1,1,3,256,512]{4,3,2,1,0:T(8,128)(2,1)} %bitcast.6) | data formatting | bytes 1572864
  57.4 0.0 copy-done.1
  57.4 1.0 %copy.22 = f32[1,128,2048]{2,1,0:T(8,128)} copy(f32[1,128,2048]{2,1,0:T(8,128)S(1)} %bitcast.5) | data formatting | bytes 2097152
  58.4 0.0 copy-done
  58.4 1.0 %copy.23 = f32[1,128,2048]{2,1,0:T(8,128)} copy(f32[1,128,2048]{2,1,0:T(8,128)S(1)} %bitcast.4) | data formatting | bytes 2097152
Async XLA Ops:
  53.1 4.3 %copy-start.1 = (f32[128,2048]{1,0:T(8,128)S(1)}, f32[128,2048]{1,0:T(8,128)}, u32[]{:S(2)}) copy-start(f32[128,2048]{1,0:T(8,128)} %get-tuple-element.10) | copy-start | bytes 3145732
  55.3 3.1 %copy-start = (f32[128,2048]{1,0:T(8,128)S(1)}, f32[128,2048]{1,0:T(8,128)}, u32[]{:S(2)}) copy-start(f32[128,2048]{1,0:T(8,128)} %get-tuple-element.11) | copy-start | bytes 3145732

commit v2 on v1

--- a/solution.py
+++ b/solution.py
@@ -23,15 +23,15 @@
 
 
 def gelu(pre, slope):
+    pre = pre.astype(BF)
     square = pre * pre
     tangent = jnp.tanh(pre * (gelu_coeff + (gelu_coeff * cubic_coeff) * square))
-    half = 0.5 * pre
-    cdf = 1.0 + tangent
-    hidden = (half * cdf).astype(BF)
+    gate = 0.5 * tangent + 0.5
+    hidden = pre * gate
     if not slope:
         return hidden, None
-    bent = gelu_coeff + (3.0 * gelu_coeff * cubic_coeff) * square
-    return hidden, 0.5 * cdf + (half * bent) * (1.0 - tangent * tangent)
+    bent = pre * (2.0 * gelu_coeff + (6.0 * gelu_coeff * cubic_coeff) * square)
+    return hidden, gate * (1.0 + bent * (1.0 - gate))
 
 
 def dot(a, b):
@@ -168,7 +168,7 @@
             f_hid[:, cols(j)] = gelu(dot(a_in[k], w1[:, cols(j)]), False)[0]
             return 0
 
-        lax.fori_loop(0, chunks, body, 0)
+        lax.fori_loop(0, chunks, body, 0, unroll=2)
         value = norm(a_in[k], dot_nt(f_hid[...], w2[...]))[0]
         live = row_ids < lengths[me, k - s + sections - 1]
         act_b[k] = jnp.where(live, value, 0.0).astype(BF)
@@ -192,7 +192,7 @@
             slopes[k, :, cols(j)] = slope
             return 0
 
-        lax.fori_loop(0, chunks, body, 0)
+        lax.fori_loop(0, chunks, body, 0, unroll=2)
         if k == 0:
             load_w2.wait()
         value, inv = norm(x_in[k], dot_nt(hid[block(k), :], w2[...]))
@@ -226,10 +226,10 @@
         normed[k] = grad_sum
 
         def body(j, _):
-            gp[block(k), cols(j)] = (dot(g_b[k], w2[:, cols(j)]) * slopes[k, :, cols(j)]).astype(BF)
+            gp[block(k), cols(j)] = dot(g_b[k], w2[:, cols(j)]).astype(BF) * slopes[k, :, cols(j)]
             return 0
 
-        lax.fori_loop(0, chunks, body, 0)
+        lax.fori_loop(0, chunks, body, 0, unroll=2)
         cot_b[k] = (residual_alpha * normed[k] + dot_nt(gp[block(k), :], w1[...])).astype(BF)
         if k + 1 < ticks:
             @pl.when(jnp.logical_not(first))
@@ -247,10 +247,10 @@
             def body(j, _):
                 hidden, slope = gelu(dot(r_x[k, p], w1[:, cols(j)]), True)
                 hid[place, cols(j)] = hidden
-                gp[place, cols(j)] = (dot(r_g[k, p], w2[:, cols(j)]) * slope).astype(BF)
+                gp[place, cols(j)] = dot(r_g[k, p], w2[:, cols(j)]).astype(BF) * slope
                 return 0
 
-            lax.fori_loop(0, chunks, body, 0)
+            lax.fori_loop(0, chunks, body, 0, unroll=2)
             xt[:, place] = r_x[k, p, :, chip_cols].T
             gt[:, place] = r_g[k, p, :, chip_cols].T
 
@@ -272,7 +272,7 @@
             acc[i, :, cols(j)] = dot(left[:, :early], right[:early, cols(j)])
             return 0
 
-        lax.fori_loop(0, chunks, body, 0)
+        lax.fori_loop(0, chunks, body, 0, unroll=2)
 
     stage_r(ticks - 1)
 
@@ -328,6 +328,25 @@
         store.wait()
 
 
+def hand_over(*refs):
+    count = len(refs) // 2
+    sem = refs[-1]
+    copies, used = [], 0
+    for src, dst in zip(refs[:count], refs[count : 2 * count]):
+        if len(src.shape) == 3:
+            spans = list(range(src.shape[0]))
+        else:
+            part = src.shape[0] // 4
+            spans = [pl.ds(i * part, part) for i in range(4)]
+        for span in spans:
+            copies.append(pltpu.make_async_copy(src.at[span], dst.at[span], sem.at[used]))
+            used += 1
+    for copy in copies:
+        copy.start()
+    for copy in copies:
+        copy.wait()
+
+
 def on_device(*args):
     w_first, lengths, stash = args[0], args[6], args[11]
     sections, groups = lax.axis_size("section"), lax.axis_size("dp")
@@ -344,7 +363,7 @@
     anywhere = pl.BlockSpec(memory_space=pl.ANY)
     leave = jax.ShapeDtypeStruct((ticks, cap, width), BF)
     step = jax.ShapeDtypeStruct((own, units), F32)
-    act, cot, step_first, step_second = pl.pallas_call(
+    made = pl.pallas_call(
         functools.partial(kernel, sections, groups, ticks, chunk),
         out_shape=(leave, leave, step, step),
         in_specs=[anywhere] * 6 + [pl.BlockSpec(memory_space=pltpu.SMEM)] + [anywhere] * 5,
@@ -361,7 +380,7 @@
             vmem((ticks, cap, width), BF),
             vmem((ticks, cap, width), BF),
             vmem((ticks, cap, width), BF),
-            vmem((ticks, cap, units), F32),
+            vmem((ticks, cap, units), BF),
             vmem((ticks, cap, width), F32),
             vmem((ticks, cap, 1), F32),
             vmem((cap, units), BF),
@@ -393,6 +412,14 @@
             collective_id=0, has_side_effects=True, vmem_limit_bytes=60 * 2**20
         ),
     )(*args)
+    act, cot, step_first, step_second = pl.pallas_call(
+        hand_over,
+        out_shape=(leave, leave, step, step),
+        in_specs=[anywhere] * 4,
+        out_specs=(anywhere,) * 4,
+        scratch_shapes=[dma((2 * ticks + 8,))],
+        compiler_params=pltpu.CompilerParams(vmem_limit_bytes=60 * 2**20),
+    )(*made)
     return act[None, None], cot[None, None], step_first[None], step_second[None]
 
 

time: 59.7 us -> 163 us (2.73)
  Pallas kernels: 52.5 us -> 160 us
  local copies, waits for them, and re-layouts: 6.25 us -> 0 us
    pallas_call x0 -> x1, Pallas kernels: none -> 112 us  [on_device(): pl.pallas_call(hand_over, out_shape=(leave, leave, step, step), in_specs=...]
    unnamed x8 -> x0, local copies, waits for them, and re-layouts: 6.25 us -> none
    pallas_call x1, Pallas kernels: 52.5 us -> 48 us  [on_device(): pl.pallas_call(functools.partial(kernel, sections, groups, ticks, chunk),...]
where the time goes in v2:
time: 163 us; the launch traced here: 161 us
  Pallas kernels  160 us (98%)
    pallas_call x1, Pallas kernels, on_device(): pl.pallas_call(hand_over, out_shape=(leave, leave, step, step), in_specs=...  112 us
    pallas_call x1, Pallas kernels, on_device(): pl.pallas_call(functools.partial(kernel, sections, groups, ticks, chunk),...  48 us

profile of v2, /device:TPU:0, one launch (start us, length us, event | category | flops | bytes accessed | tf_op | source)
XLA Modules:
  0.0 161.2 jit_solution(1590502622731961620)
XLA Ops:
  0.6 48.0 %shard_map.147 = (bf16[3,256,512]{2,1,0:T(8,128)(2,1)}, bf16[3,256,512]{2,1,0:T(8,128)(2,1)}, f32[128,2048]{1,0:T(8,128)}, f32[128,2048]{1,0:T(8,128)}) custom-call(bf16[1,512,2048]{2,1,0:T(8,128)(2,1)} %w1_h.1, bf16[1,512,2048]{2,1,0:T(8,128)(2,1)} %w2_h.1, f32[1,128,2048]{2,1,0:T(8,128)} %m1_h.1, f32[1,128,2048]{2,1,0:T(8,128)} %v1_h.1, ...), custom_call_target="tpu_custom_call" | custom-call | tf_op jit(solution)/shard_map/pallas_call | solution.py:366
  48.7 112.4 %shard_map.148 = (bf16[3,256,512]{2,1,0:T(8,128)(2,1)}, bf16[3,256,512]{2,1,0:T(8,128)(2,1)}, f32[128,2048]{1,0:T(8,128)}, f32[128,2048]{1,0:T(8,128)}) custom-call(bf16[3,256,512]{2,1,0:T(8,128)(2,1)} %get-tuple-element.12.refs_0_, bf16[3,256,512]{2,1,0:T(8,128)(2,1)} %get-tuple-element.13.refs_1_, f32[128,2048]{1,0:T(8,128)} %get-tuple-element.14.refs_2_, ...), custom_call_target="tpu_custom_call" | custom-call | tf_op jit(solution)/shard_map/pallas_call | solution.py:415

commit v3 on v2

--- a/solution.py
+++ b/solution.py
@@ -46,7 +46,7 @@
     sections, groups, ticks, chunk,
     w1_h, w2_h, m1_h, v1_h, m2_h, v2_h, lengths, act_h, cot_h, embed_h, loss_h, stash_h,
     act_o, cot_o, s1_o, s2_o,
-    w1, w2, moments, x_in, a_in, c_in, r_x, r_g, act_b, cot_b, g_b, slopes, normed, inv_std,
+    w1, w2, moments, x_in, a_in, c_in, r_x, r_g, act_b, cot_b, g_b, slopes, r_slope, normed, inv_std,
     f_hid, hid, gp, xt, gt, acc, out_x, in_x, steps,
     w_sem, mom_sem, x_sem, a_sem, c_sem, o_sem, st_sem,
     hop_s, hop_r, rx_s, rx_r, rg_s, rg_r, ex_s, ex_r,
@@ -127,9 +127,8 @@
 
     sends_x = [send_tick(k, stash_h.at[0, 0, k], r_x, rx_s, rx_r) for k in range(ticks)]
     sends_g = [send_tick(k, g_b.at[k], r_g, rg_s, rg_r) for k in range(ticks)]
-    for copies in sends_x:
-        for copy in copies:
-            copy.start()
+    for copy in sends_x[0]:
+        copy.start()
 
     def hop(src, dst, i, to):
         return pltpu.make_async_remote_copy(
@@ -221,7 +220,7 @@
             - value * jnp.mean(grad_out * value, axis=1, keepdims=True)
         )
         g_b[k] = grad_sum.astype(BF)
-        for copy in sends_g[k]:
+        for copy in sends_g[k] + (sends_x[k + 1] if k + 1 < ticks else []):
             copy.start()
         normed[k] = grad_sum
 
@@ -238,21 +237,29 @@
         outs_c[k].start()
         gt[:, block(k)] = g_b[k, :, chip_cols].T
 
-    def stage_r(k):
+    def place(k, p):
+        return block(ticks + k * (chips - 1) + p)
+
+    def stage_rx(k):
         for p in range(chips - 1):
             sends_x[k][p].wait_recv()
-            sends_g[k][p].wait_recv()
-            place = block(ticks + k * (chips - 1) + p)
 
             def body(j, _):
                 hidden, slope = gelu(dot(r_x[k, p], w1[:, cols(j)]), True)
-                hid[place, cols(j)] = hidden
-                gp[place, cols(j)] = dot(r_g[k, p], w2[:, cols(j)]).astype(BF) * slope
+                hid[place(k, p), cols(j)] = hidden
+                r_slope[p, :, cols(j)] = slope
                 return 0
 
             lax.fori_loop(0, chunks, body, 0, unroll=2)
-            xt[:, place] = r_x[k, p, :, chip_cols].T
-            gt[:, place] = r_g[k, p, :, chip_cols].T
+            xt[:, place(k, p)] = r_x[k, p, :, chip_cols].T
+
+    def stage_rg(k):
+        for p in range(chips - 1):
+            sends_g[k][p].wait_recv()
+            gt[:, place(k, p)] = r_g[k, p, :, chip_cols].T
+
+    def remote_gp(k, p, span):
+        gp[place(k, p), span] = dot(r_g[k, p], w2[:, span]).astype(BF) * r_slope[p, :, span]
 
     early = (ticks + (ticks - 1) * (chips - 1)) * cap
     terms = ((xt, gp), (gt, hid))
@@ -263,9 +270,17 @@
     for k in range(1, ticks):
         stage_a(k)
     for k in range(1, ticks):
+        stage_rx(k - 1)
         stage_b(k)
-        stage_r(k - 1)
+        stage_rg(k - 1)
+        for p in range(chips - 1):
+            def body(j, _):
+                remote_gp(k - 1, p, cols(j))
+                return 0
+
+            lax.fori_loop(0, chunks, body, 0, unroll=2)
         forward(k)
+    stage_rx(ticks - 1)
 
     for i, (left, right) in enumerate(terms):
         def body(j, _):
@@ -274,13 +289,15 @@
 
         lax.fori_loop(0, chunks, body, 0, unroll=2)
 
-    stage_r(ticks - 1)
+    stage_rg(ticks - 1)
 
     swaps = []
     theirs = pl.ds(pl.multiple_of((1 - core) * own, own), own)
     mine = pl.ds(pl.multiple_of(core * own, own), own)
     for j in range(chunks):
         span = slice(j * chunk, (j + 1) * chunk)
+        for p in range(chips - 1):
+            remote_gp(ticks - 1, p, span)
         for i, (left, right) in enumerate(terms):
             if chips > 1:
                 acc[i, :, span] += dot(left[:, early:], right[early:, span])
@@ -329,22 +346,24 @@
 
 
 def hand_over(*refs):
-    count = len(refs) // 2
-    sem = refs[-1]
-    copies, used = [], 0
-    for src, dst in zip(refs[:count], refs[count : 2 * count]):
+    sources, results, held, sems = refs[:4], refs[4:8], refs[8:12], refs[12]
+    loads, stores = [], []
+    for src, dst, buf in zip(sources, results, held):
         if len(src.shape) == 3:
             spans = list(range(src.shape[0]))
         else:
             part = src.shape[0] // 4
             spans = [pl.ds(i * part, part) for i in range(4)]
         for span in spans:
-            copies.append(pltpu.make_async_copy(src.at[span], dst.at[span], sem.at[used]))
-            used += 1
-    for copy in copies:
-        copy.start()
-    for copy in copies:
-        copy.wait()
+            loads.append(pltpu.make_async_copy(src.at[span], buf.at[span], sems.at[0, len(loads)]))
+            stores.append(pltpu.make_async_copy(buf.at[span], dst.at[span], sems.at[1, len(stores)]))
+    for load in loads:
+        load.start()
+    for load, store in zip(loads, stores):
+        load.wait()
+        store.start()
+    for store in stores:
+        store.wait()
 
 
 def on_device(*args):
@@ -381,6 +400,7 @@
             vmem((ticks, cap, width), BF),
             vmem((ticks, cap, width), BF),
             vmem((ticks, cap, units), BF),
+            vmem((max(chips - 1, 1), cap, units), BF),
             vmem((ticks, cap, width), F32),
             vmem((ticks, cap, 1), F32),
             vmem((cap, units), BF),
@@ -417,7 +437,13 @@
         out_shape=(leave, leave, step, step),
         in_specs=[anywhere] * 4,
         out_specs=(anywhere,) * 4,
-        scratch_shapes=[dma((2 * ticks + 8,))],
+        scratch_shapes=[
+            vmem(leave.shape, BF),
+            vmem(leave.shape, BF),
+            vmem(step.shape, F32),
+            vmem(step.shape, F32),
+            dma((2, 2 * ticks + 8)),
+        ],
         compiler_params=pltpu.CompilerParams(vmem_limit_bytes=60 * 2**20),
     )(*made)
     return act[None, None], cot[None, None], step_first[None], step_second[None]

time: 163 us -> 52.3 us (0.32)
  the two profiles are of different devices: /device:TPU:0 before, /device:TPU:21 now
where the time goes in v3:
time: 52.3 us; the launch traced here: 52.1 us
  Pallas kernels  51.3 us (98%)
  between operations  0.8 us (2%)
    pallas_call x1, Pallas kernels, on_device(): pl.pallas_call(functools.partial(kernel, sections, groups, ticks, chunk),...  48 us
    pallas_call x1, Pallas kernels, on_device(): pl.pallas_call(hand_over, out_shape=(leave, leave, step, step), in_specs=...  3.26 us

profile of v3, /device:TPU:21, one launch (start us, length us, event | category | flops | bytes accessed | tf_op | source)
XLA Modules:
  0.0 52.1 jit_solution(15775762343740039332)
XLA Ops:
  0.6 48.0 %shard_map.147 = (bf16[3,256,512]{2,1,0:T(8,128)(2,1)}, bf16[3,256,512]{2,1,0:T(8,128)(2,1)}, f32[128,2048]{1,0:T(8,128)}, f32[128,2048]{1,0:T(8,128)}) custom-call(bf16[1,512,2048]{2,1,0:T(8,128)(2,1)} %w1_h.1, bf16[1,512,2048]{2,1,0:T(8,128)(2,1)} %w2_h.1, f32[1,128,2048]{2,1,0:T(8,128)} %m1_h.1, f32[1,128,2048]{2,1,0:T(8,128)} %v1_h.1, ...), custom_call_target="tpu_custom_call" | custom-call | tf_op jit(solution)/shard_map/pallas_call | solution.py:385
  48.7 3.3 %shard_map.148 = (bf16[3,256,512]{2,1,0:T(8,128)(2,1)}, bf16[3,256,512]{2,1,0:T(8,128)(2,1)}, f32[128,2048]{1,0:T(8,128)}, f32[128,2048]{1,0:T(8,128)}) custom-call(bf16[3,256,512]{2,1,0:T(8,128)(2,1)} %get-tuple-element.12.refs_0_, bf16[3,256,512]{2,1,0:T(8,128)(2,1)} %get-tuple-element.13.refs_1_, f32[128,2048]{1,0:T(8,128)} %get-tuple-element.14.refs_2_, ...), custom_call_target="tpu_custom_call" | custom-call | tf_op jit(solution)/shard_map/pallas_call | solution.py:435

commit v4 on v3

--- a/solution.py
+++ b/solution.py
@@ -264,23 +264,29 @@
     early = (ticks + (ticks - 1) * (chips - 1)) * cap
     terms = ((xt, gp), (gt, hid))
 
+    def remote_products(k):
+        for p in range(chips - 1):
+            def body(j, _):
+                remote_gp(k, p, cols(j))
+                return 0
+
+            lax.fori_loop(0, chunks, body, 0, unroll=2)
+
     stage_a(0)
     stage_b(0)
-    forward(0)
     for k in range(1, ticks):
         stage_a(k)
-    for k in range(1, ticks):
+    forward(0)
+    stage_b(1)
+    stage_rx(0)
+    for k in range(2, ticks):
+        stage_rg(k - 2)
+        remote_products(k - 2)
         stage_rx(k - 1)
+        forward(k - 1)
         stage_b(k)
-        stage_rg(k - 1)
-        for p in range(chips - 1):
-            def body(j, _):
-                remote_gp(k - 1, p, cols(j))
-                return 0
-
-            lax.fori_loop(0, chunks, body, 0, unroll=2)
-        forward(k)
-    stage_rx(ticks - 1)
+    stage_rg(ticks - 2)
+    remote_products(ticks - 2)
 
     for i, (left, right) in enumerate(terms):
         def body(j, _):
@@ -289,6 +295,8 @@
 
         lax.fori_loop(0, chunks, body, 0, unroll=2)
 
+    stage_rx(ticks - 1)
+    forward(ticks - 1)
     stage_rg(ticks - 1)
 
     swaps = []

time: 52.3 us -> 49.1 us (0.939)
  the two profiles are of different devices: /device:TPU:21 before, /device:TPU:0 now
where the time goes in v4:
time: 49.1 us; the launch traced here: 48.9 us
  Pallas kernels  48.1 us (98%)
  between operations  0.8 us (2%)
    pallas_call x1, Pallas kernels, on_device(): pl.pallas_call(functools.partial(kernel, sections, groups, ticks, chunk),...  44.9 us
    pallas_call x1, Pallas kernels, on_device(): pl.pallas_call(hand_over, out_shape=(leave, leave, step, step), in_specs=...  3.26 us

profile of v4, /device:TPU:0, one launch (start us, length us, event | category | flops | bytes accessed | tf_op | source)
XLA Modules:
  0.0 48.9 jit_solution(10778877542650196471)
XLA Ops:
  0.6 44.9 %shard_map.147 = (bf16[3,256,512]{2,1,0:T(8,128)(2,1)}, bf16[3,256,512]{2,1,0:T(8,128)(2,1)}, f32[128,2048]{1,0:T(8,128)}, f32[128,2048]{1,0:T(8,128)}) custom-call(bf16[1,512,2048]{2,1,0:T(8,128)(2,1)} %w1_h.1, bf16[1,512,2048]{2,1,0:T(8,128)(2,1)} %w2_h.1, f32[1,128,2048]{2,1,0:T(8,128)} %m1_h.1, f32[1,128,2048]{2,1,0:T(8,128)} %v1_h.1, ...), custom_call_target="tpu_custom_call" | custom-call | tf_op jit(solution)/shard_map/pallas_call | solution.py:393
  45.5 3.3 %shard_map.148 = (bf16[3,256,512]{2,1,0:T(8,128)(2,1)}, bf16[3,256,512]{2,1,0:T(8,128)(2,1)}, f32[128,2048]{1,0:T(8,128)}, f32[128,2048]{1,0:T(8,128)}) custom-call(bf16[3,256,512]{2,1,0:T(8,128)(2,1)} %get-tuple-element.12.refs_0_, bf16[3,256,512]{2,1,0:T(8,128)(2,1)} %get-tuple-element.13.refs_1_, f32[128,2048]{1,0:T(8,128)} %get-tuple-element.14.refs_2_, ...), custom_call_target="tpu_custom_call" | custom-call | tf_op jit(solution)/shard_map/pallas_call | solution.py:443

commit v5 on v4

--- a/solution.py
+++ b/solution.py
@@ -220,7 +220,7 @@
             - value * jnp.mean(grad_out * value, axis=1, keepdims=True)
         )
         g_b[k] = grad_sum.astype(BF)
-        for copy in sends_g[k] + (sends_x[k + 1] if k + 1 < ticks else []):
+        for copy in sends_g[k] + (sum(sends_x[1:], []) if k == 0 else []):
             copy.start()
         normed[k] = grad_sum
 

time: 49.1 us -> 52.3 us (1.065)
  Pallas kernels: 48.1 us -> 51.3 us
    pallas_call x1, Pallas kernels: 44.9 us -> 48 us  [on_device(): pl.pallas_call(functools.partial(kernel, sections, groups, ticks, chunk),...]
where the time goes in v5:
time: 52.3 us; the launch traced here: 52.1 us
  Pallas kernels  51.3 us (98%)
  between operations  0.8 us (2%)
    pallas_call x1, Pallas kernels, on_device(): pl.pallas_call(functools.partial(kernel, sections, groups, ticks, chunk),...  48 us
    pallas_call x1, Pallas kernels, on_device(): pl.pallas_call(hand_over, out_shape=(leave, leave, step, step), in_specs=...  3.26 us

profile of v5, /device:TPU:0, one launch (start us, length us, event | category | flops | bytes accessed | tf_op | source)
XLA Modules:
  0.0 52.1 jit_solution(3044867552685575046)
XLA Ops:
  0.6 48.0 %shard_map.147 = (bf16[3,256,512]{2,1,0:T(8,128)(2,1)}, bf16[3,256,512]{2,1,0:T(8,128)(2,1)}, f32[128,2048]{1,0:T(8,128)}, f32[128,2048]{1,0:T(8,128)}) custom-call(bf16[1,512,2048]{2,1,0:T(8,128)(2,1)} %w1_h.1, bf16[1,512,2048]{2,1,0:T(8,128)(2,1)} %w2_h.1, f32[1,128,2048]{2,1,0:T(8,128)} %m1_h.1, f32[1,128,2048]{2,1,0:T(8,128)} %v1_h.1, ...), custom_call_target="tpu_custom_call" | custom-call | tf_op jit(solution)/shard_map/pallas_call | solution.py:393
  48.7 3.3 %shard_map.148 = (bf16[3,256,512]{2,1,0:T(8,128)(2,1)}, bf16[3,256,512]{2,1,0:T(8,128)(2,1)}, f32[128,2048]{1,0:T(8,128)}, f32[128,2048]{1,0:T(8,128)}) custom-call(bf16[3,256,512]{2,1,0:T(8,128)(2,1)} %get-tuple-element.12.refs_0_, bf16[3,256,512]{2,1,0:T(8,128)(2,1)} %get-tuple-element.13.refs_1_, f32[128,2048]{1,0:T(8,128)} %get-tuple-element.14.refs_2_, ...), custom_call_target="tpu_custom_call" | custom-call | tf_op jit(solution)/shard_map/pallas_call | solution.py:443
